TPU v7x, 256 devices: a whole 4x4x8 slice. The times are simulated.
256 devices in a mesh: ctx: 64 (over y_lo, z, x), head: 4 (over y_hi, core).
Axes of the slice: x: 4, y: 4 (y_hi: 2, y_lo: 2; y = y_hi * 2 + y_lo), z: 8, core: 2. Of those that a mesh axis runs over, the one named last changes fastest.
Arguments:
- queries: bfloat16 [32768, 2048], P('ctx', 'head'), may hold values from -30 to 30
- key_rows: bfloat16 [32768, 2048], P('ctx', 'head'), may hold values from -6 to 6
- value_rows: bfloat16 [32768, 2048], P('ctx', 'head'), may hold values from -6 to 6
Outputs:
- attended: bfloat16 [32768, 2048], P(('ctx', 'head'))
All inputs are finite; a program needn't handle non-finite values.
Results may differ from a plain program's by a relative error of at most 0.0041.
Values may be sent and summed in bfloat16 or wider, within the bound.
A program may use at most 128 MiB of HBM per device.

v0:
```python
import jax
import jax.numpy as jnp
from jax import lax
from jax.sharding import PartitionSpec as P

HD = 128
WINDOW = 1024
STRIDE = 2048
SUMM = 16


def shifted(block, axis, distance):
    devices = range(lax.axis_size(axis))
    route = [(i - distance, i) for i in devices if i - distance in devices]
    return lax.ppermute(block, axis, route)


def on_device(queries, key_rows, value_rows):
    tok_rows = queries.shape[0]
    feat_width = queries.shape[1]
    local_heads = feat_width // HD
    score_scale = HD ** (-0.5)
    ctx_count = lax.axis_size("ctx")
    ctx_place = lax.axis_index("ctx")
    first_pos = ctx_place * tok_rows
    halo_hops = max(1, WINDOW // tok_rows)
    key_parts = []
    value_parts = []
    for distance in range(halo_hops, 0, -1):
        moved_keys, moved_values = shifted((key_rows, value_rows), "ctx", distance)
        key_parts.append(moved_keys)
        value_parts.append(moved_values)
    keys_ext = jnp.concatenate(key_parts + [key_rows], axis=0)
    values_ext = jnp.concatenate(value_parts + [value_rows], axis=0)
    segment = min(tok_rows, STRIDE)
    groups = tok_rows // segment
    slot_count = groups * SUMM
    own_keys = key_rows.reshape(groups, segment, feat_width)[:, segment - SUMM :].reshape(
        slot_count, feat_width
    )
    own_values = value_rows.reshape(groups, segment, feat_width)[:, segment - SUMM :].reshape(
        slot_count, feat_width
    )
    slot_index = jnp.arange(ctx_count * slot_count, dtype=jnp.int32)
    summ_keys, summ_values = (
        lax.all_gather(own_keys, "ctx", axis=0, tiled=True),
        lax.all_gather(own_values, "ctx", axis=0, tiled=True),
    )
    source_dev = slot_index // slot_count
    within_dev = slot_index % slot_count
    summ_pos = (
        source_dev * tok_rows + within_dev // SUMM * segment + (segment - SUMM) + within_dev % SUMM
    )
    summ_real = (summ_pos % STRIDE >= STRIDE - SUMM) & (source_dev >= 0)
    summ_keys3 = summ_keys.reshape(-1, local_heads, HD)
    summ_values3 = summ_values.reshape(-1, local_heads, HD)
    blk_rows = min(512, tok_rows)
    query_blk = queries.reshape(blk_rows, local_heads, HD)
    key_slab = keys_ext.reshape(blk_rows + WINDOW, local_heads, HD)
    value_slab = values_ext.reshape(blk_rows + WINDOW, local_heads, HD)
    query_pos = first_pos + 0 + jnp.arange(blk_rows, dtype=jnp.int32)
    key_pos = first_pos + 0 - WINDOW + jnp.arange(blk_rows + WINDOW, dtype=jnp.int32)
    near_mask = (
        (key_pos[None, :] <= query_pos[:, None])
        & (query_pos[:, None] - key_pos[None, :] < WINDOW)
        & (key_pos[None, :] >= 0)
    )
    far_mask = (summ_pos[None, :] <= query_pos[:, None] - WINDOW) & summ_real[None, :]
    near_scores = (
        jnp.einsum("qhd,khd->hqk", query_blk, key_slab, preferred_element_type=jnp.float32)
        * score_scale
    )
    near_scores = jnp.where(near_mask[None], near_scores, -jnp.inf)
    far_scores = (
        jnp.einsum("qhd,khd->hqk", query_blk, summ_keys3, preferred_element_type=jnp.float32)
        * score_scale
    )
    far_scores = jnp.where(far_mask[None], far_scores, -jnp.inf)
    row_max = jnp.maximum(jnp.max(near_scores, axis=-1), jnp.max(far_scores, axis=-1))
    near_weights = jnp.exp(near_scores - row_max[..., None])
    far_weights = jnp.exp(far_scores - row_max[..., None])
    weight_sum = jnp.sum(near_weights, axis=-1) + jnp.sum(far_weights, axis=-1)
    mixed = jnp.einsum(
        "hqk,khd->qhd",
        near_weights.astype(jnp.bfloat16),
        value_slab,
        preferred_element_type=jnp.float32,
    )
    mixed = mixed + jnp.einsum(
        "hqk,khd->qhd",
        far_weights.astype(jnp.bfloat16),
        summ_values3,
        preferred_element_type=jnp.float32,
    )
    outputs = (
        (mixed / jnp.transpose(weight_sum)[:, :, None])
        .astype(jnp.bfloat16)
        .reshape(blk_rows, feat_width)
    )
    return lax.all_to_all(outputs, "head", split_axis=0, concat_axis=1, tiled=True)


def solution(mesh):
    placed = (P("ctx", "head"), P("ctx", "head"), P("ctx", "head"))
    return jax.shard_map(
        on_device, mesh=mesh, in_specs=placed, out_specs=P(("ctx", "head"), None), check_vma=False
    )
```

profile of v0, /device:TPU:1, one launch (start us, length us, event | category | flops | bytes accessed | tf_op | source)
XLA Modules:
  0.0 648.8 jit_solution(8580374890728359577)
XLA Ops:
  6.5 1.4 slice.8
  8.0 2.0 copy.25
  10.0 6.3 collective-permute-start.2
  16.3 3.0 collective-permute-start.3
  19.3 3.5 collective-permute-start
  22.8 3.9 collective-permute-start.1
  26.7 1.3 slice.9
  29.8 20.1 %collective-permute-done = bf16[512,512]{1,0:T(8,128)(2,1)S(1)} collective-permute-done((bf16[512,512]{1,0:T(8,128)(2,1)}, bf16[512,512]{1,0:T(8,128)(2,1)S(1)}, u32[]{:S(2)}, u32[]{:S(2)}) %collective-permute-start) | collective-permute-done | bytes 524320 | tf_op jit(solution)/shard_map/ppermute | solution.py:15
  50.7 10.9 %collective-permute-done.1 = bf16[512,512]{1,0:T(8,128)(2,1)} collective-permute-done((bf16[512,512]{1,0:T(8,128)(2,1)}, bf16[512,512]{1,0:T(8,128)(2,1)}, u32[]{:S(2)}, u32[]{:S(2)}) %collective-permute-start.1) | collective-permute-done | bytes 524320 | tf_op jit(solution)/shard_map/ppermute | solution.py:15
  61.5 1.5 pad_maximum_fusion
  63.0 1.6 copy.24
  64.6 1.5 pad_maximum_fusion.1
  66.1 6.0 fusion.2
  72.1 200.8 %all-gather.5.cloned.1.call-done = bf16[1,1024,512]{2,1,0:T(8,128)(2,1)} async-done(((bf16[1,16,512]{2,1,0:T(8,128)(2,1)}), bf16[1,1024,512]{2,1,0:T(8,128)(2,1)}) %all-gather.5.cloned.1.call-update) | async-done | bytes 1048592 | tf_op jit(solution)/shard_map/all_gather | solution.py:46
  272.9 1.5 copy.30
  274.4 1.7 fusion.3
  276.1 4.2 copy-done.2
  280.4 2.4 fusion.4
  282.8 2.8 fusion
  285.6 280.8 %all-gather.7.cloned.1.call-done = bf16[1,1024,512]{2,1,0:T(8,128)(2,1)} async-done(((bf16[1,16,512]{2,1,0:T(8,128)(2,1)}), bf16[1,1024,512]{2,1,0:T(8,128)(2,1)}) %all-gather.7.cloned.1.call-update) | async-done | bytes 1048592 | tf_op jit(solution)/shard_map/all_gather | solution.py:47
  566.4 2.2 copy.34
  568.6 4.9 fusion.14
  573.6 8.2 %divide_convert_fusion = bf16[512,4,128]{0,2,1:T(8,128)(2,1)S(1)} fusion(f32[512,4,128]{0,2,1:T(8,128)S(1)} %fusion.14, bf16[1536,4,128]{0,2,1:T(8,128)(2,1)S(1)} %bitcast.59, f32[4,1536,512]{2,1,0:T(8,128)} %get-tuple-element.6, f32[4,512]{1,0:T(4,128)S(1)} %max.7, pred[512,1536]{0,1:T(8,128)(4,1)S(1)} %fusion.13, f32[512,4]{0,1:T(4,128)S(1)} %add_bitcast_fusion), kind=kOutput, calls=%fused_computation.23 | convolution fusion | flops 818675712 | bytes 16531456 | tf_op jit(solution)/shard_map/hqk,khd->qhd/dot_general | solution.py:83
  582.0 58.9 %all_to_all.19 = bf16[4,128,512]{1,2,0:T(8,128)(2,1)S(1)} all-to-all(bf16[4,128,512]{1,2,0:T(8,128)(2,1)S(1)} %copy.37), channel_id=1, replica_groups=mesh['ctx'=64,'head'=4] {'head'}, dimensions={0} | all-to-all | bytes 1048576 | tf_op jit(solution)/shard_map/all_to_all | solution.py:100
  (28 shorter events, 3.8 us)
Async XLA Ops:
  6.5 59.5 %copy-start = (bf16[512,512]{1,0:T(8,128)(2,1)S(1)}, bf16[512,512]{1,0:T(8,128)(2,1)}, u32[]{:S(2)}) copy-start(bf16[512,512]{1,0:T(8,128)(2,1)} %param.3) | copy-start | bytes 1572868
  6.5 266.3 %all-gather.5.cloned.1.call-start = ((), (), s32[]{:S(2)}) async-start(), calls=%async_computation.1 | async-start | bytes 1064960 | tf_op jit(solution)/shard_map/all_gather | solution.py:46
  7.9 558.5 %all-gather.7.cloned.1.call-start = ((), (), s32[]{:S(2)}) async-start(), calls=%async_computation.2 | async-start | bytes 1064960 | tf_op jit(solution)/shard_map/all_gather | solution.py:47
  10.0 54.5 %collective-permute-start.2 = (bf16[512,512]{0,1:T(8,128)(2,1)}, bf16[512,512]{0,1:T(8,128)(2,1)}, u32[]{:S(2)}, u32[]{:S(2)}) collective-permute-start(bf16[512,512]{0,1:T(8,128)(2,1)} %copy.25), channel_id=1, source_target_pairs={{0,8},{4,12},{8,16},{12,20},{16,24},{20,28},{24,32},{28,36},{32,40... | collective-permute-start | bytes 1572872 | tf_op jit(solution)/shard_map/ppermute | solution.py:15
  16.3 48.3 %collective-permute-start.3 = (bf16[512,512]{0,1:T(8,128)(2,1)}, bf16[512,512]{0,1:T(8,128)(2,1)}, u32[]{:S(2)}, u32[]{:S(2)}) collective-permute-start(bf16[512,512]{0,1:T(8,128)(2,1)} %copy.25), channel_id=1, source_target_pairs={{0,4},{4,8},{8,12},{12,16},{16,20},{20,24},{24,28},{28,32},{32,36}... | collective-permute-start | bytes 1572872 | tf_op jit(solution)/shard_map/ppermute | solution.py:15
  19.3 30.5 %collective-permute-start = (bf16[512,512]{1,0:T(8,128)(2,1)}, bf16[512,512]{1,0:T(8,128)(2,1)S(1)}, u32[]{:S(2)}, u32[]{:S(2)}) collective-permute-start(bf16[512,512]{1,0:T(8,128)(2,1)} %param.5), channel_id=1, source_target_pairs={{0,8},{4,12},{8,16},{12,20},{16,24},{20,28},{24,32},{28,36},{32,40... | collective-permute-start | bytes 1572872 | tf_op jit(solution)/shard_map/ppermute | solution.py:15
  22.8 38.8 %collective-permute-start.1 = (bf16[512,512]{1,0:T(8,128)(2,1)}, bf16[512,512]{1,0:T(8,128)(2,1)}, u32[]{:S(2)}, u32[]{:S(2)}) collective-permute-start(bf16[512,512]{1,0:T(8,128)(2,1)} %param.5), channel_id=1, source_target_pairs={{0,4},{4,8},{8,12},{12,16},{16,20},{20,24},{24,28},{28,32},{32,36}... | collective-permute-start | bytes 1572872 | tf_op jit(solution)/shard_map/ppermute | solution.py:15
  49.8 0.8 copy-start.4
  274.4 8.4 %copy-start.1 = (f32[4,1536,512]{2,1,0:T(8,128)S(1)}, f32[4,1536,512]{2,1,0:T(8,128)}, u32[]{:S(2)}) copy-start(f32[4,1536,512]{2,1,0:T(8,128)} %get-tuple-element.6) | copy-start | bytes 37748740
  276.1 4.3 copy-start.2
  285.5 288.1 %copy-start.3 = (bf16[1536,512]{0,1:T(8,128)(2,1)S(1)}, bf16[1536,512]{0,1:T(8,128)(2,1)}, u32[]{:S(2)}) copy-start(bf16[1536,512]{0,1:T(8,128)(2,1)} %copy.24) | copy-start | bytes 4718596
Sparse Core Ops, SparseCore 0:
  9.1 263.6 all-gather.4
  274.7 291.7 all-gather.6
where the time goes:
time: 649 us
  waiting for transfers between devices  513 us (79%)
  blocking collectives  58.9 us (9%)
  matrix products  20.9 us (3%)
  starting transfers between devices  16.7 us (3%)
  local copies, waits for them, and re-layouts  16.3 us (3%)
  between operations  13.6 us (2%)
  other arithmetic  9.75 us (2%)
    all_gather x1, waiting for transfers between devices, on_device(): lax.all_gather(own_values, 'ctx', axis=0, tiled=True)  281 us
    all_gather x1, waiting for transfers between devices, on_device(): lax.all_gather(own_keys, 'ctx', axis=0, tiled=True)  201 us
    all_to_all x1, blocking collectives, on_device(): lax.all_to_all(outputs, 'head', split_axis=0, concat_axis=1, tiled=True)  58.9 us
    ppermute x4, waiting for transfers between devices, shifted(): return lax.ppermute(block, axis, route)  31 us
    ppermute x4, starting transfers between devices, shifted(): return lax.ppermute(block, axis, route)  16.7 us
  transfers between devices with their start and end apart: 6, of which 4 were waited for; matrix products, arithmetic and copies ran while one was open for 4% of the time, Pallas kernels for 0%

commit v1 on v0

v1 whole, which is shorter than its diff:
```python
import jax
import jax.numpy as jnp
from jax import lax
from jax.experimental import pallas as pl
from jax.experimental.pallas import tpu as pltpu
from jax.sharding import PartitionSpec as P

HD = 128
BLK = 512
RING = 4
HEAD_DEV = 4
ROWS = RING * BLK
WINDOW = 1024
SUMM = 16
GROUPS = 16
FAR = GROUPS * SUMM
TILE = 128
BAND = WINDOW + TILE
STEPS = ROWS // TILE
PIECES = 4
PIECE = BLK // PIECES
PEERS = (1, 3, 2)
LOW = -1e30
EXP_SCALE = HD**-0.5 * 1.4426950408889634
MESH = pl.DeviceIdType.MESH


def kernel(
    q_in, k_in, v_in, out, stage, q_all, kv, far, o_all, bias,
    stage_sem, kv_sem, q_sem, halo_sem, far_sem, o_sem, send_sem, halo_send, far_send, o_send,
):
    ctx, h = lax.axis_index("ctx"), lax.axis_index("head")
    x, group = lax.rem(ctx, RING), ctx // RING
    first = ctx - x

    def ring(dx):
        return lax.rem(x + dx + RING, RING)

    def group_peer(d):
        return (lax.rem(ctx + RING * d, RING * GROUPS), h)

    def cols(place):
        return pl.ds(pl.multiple_of(place * HD, HD), HD)

    def rows(start, size):
        return pl.ds(pl.multiple_of(start, TILE), size)

    def wait(ref, sem):
        pltpu.make_async_copy(ref, ref, sem).wait()

    def piece_of(dr):
        return lax.rem(h + dr, HEAD_DEV)

    staging = [
        pltpu.make_async_copy(src, stage.at[i], stage_sem.at[i])
        for i, src in ((0, k_in), (1, v_in), (2, q_in))
    ]
    for copy in staging:
        copy.start()

    barrier = pltpu.get_barrier_semaphore()
    partners = 0
    for dx in range(RING):
        for dh in range(HEAD_DEV):
            if dx or dh:
                pl.semaphore_signal(
                    barrier, inc=1, device_id=(first + ring(dx), lax.rem(h + dh, HEAD_DEV)),
                    device_id_type=MESH,
                )
                partners += 1
    for d in range(1, GROUPS):
        pl.semaphore_signal(barrier, inc=1, device_id=group_peer(d), device_id_type=MESH)
        partners += 1

    col = lax.broadcasted_iota(jnp.int32, (TILE, FAR), 1)
    row = lax.broadcasted_iota(jnp.int32, (TILE, FAR), 0)
    known = (col >= SUMM) & (col < SUMM * (group + 1))
    for case in range(3):
        seen = known
        if case == 0:
            seen = known & (col >= 2 * SUMM)
        if case == 1:
            seen = known & ((col >= 2 * SUMM) | (col - SUMM <= row - (TILE - SUMM)))
        bias[case] = jnp.where(seen, 0.0, LOW)
    far[:, 0:SUMM, :] = jnp.zeros((2, SUMM, HD), jnp.bfloat16)

    pl.semaphore_wait(barrier, partners)

    for copy in staging:
        copy.wait()
    own_kv = rows(WINDOW + x * BLK, BLK)
    pltpu.make_async_copy(stage.at[pl.ds(0, 2), :, cols(x)], kv.at[:, own_kv], kv_sem.at[x, 0]).start()
    for p in range(PIECES):
        for dx in PEERS:
            place = ring(dx)
            span = pl.ds(p * PIECE, PIECE)
            pltpu.make_async_remote_copy(
                src_ref=stage.at[pl.ds(0, 2), span, cols(place)],
                dst_ref=kv.at[:, rows(WINDOW + x * BLK + p * PIECE, PIECE)],
                send_sem=send_sem.at[0],
                recv_sem=kv_sem.at[x, p],
                device_id=(first + place, h),
                device_id_type=MESH,
            ).start()
    for dr in range(PIECES):
        r = piece_of(dr)
        span = rows(r * PIECE, PIECE)
        pltpu.make_async_copy(
            stage.at[2, span, cols(x)], q_all.at[rows(x * BLK + r * PIECE, PIECE)], q_sem.at[0, dr]
        ).start()
        for dx in PEERS:
            place = ring(dx)
            pltpu.make_async_remote_copy(
                src_ref=stage.at[2, span, cols(place)],
                dst_ref=q_all.at[rows(x * BLK + r * PIECE, PIECE)],
                send_sem=send_sem.at[1],
                recv_sem=q_sem.at[dx, dr],
                device_id=(first + place, h),
                device_id_type=MESH,
            ).start()

    def arrived(j, p):
        wait(kv.at[:, pl.ds(0, PIECE)], kv_sem.at[j, p])

    @pl.when(x >= 2)
    def _():
        wait(kv.at[:, pl.ds(0, BLK)], kv_sem.at[x, 0])

    for p in range(PIECES):
        for j in (2, 3):
            @pl.when(x != j)
            def _():
                arrived(j, p)

            pltpu.make_async_remote_copy(
                src_ref=kv.at[:, pl.ds(WINDOW + j * BLK + p * PIECE, PIECE)],
                dst_ref=kv.at[:, pl.ds((j - 2) * BLK + p * PIECE, PIECE)],
                send_sem=halo_send,
                recv_sem=halo_sem,
                device_id=group_peer(1),
                device_id_type=MESH,
            ).start()
    for d in range(1, GROUPS):
        pltpu.make_async_remote_copy(
            src_ref=kv.at[:, pl.ds(WINDOW + ROWS - SUMM, SUMM)],
            dst_ref=far.at[:, pl.ds(d * SUMM, SUMM)],
            send_sem=far_send,
            recv_sem=far_sem,
            device_id=group_peer(d),
            device_id_type=MESH,
        ).start()

    @pl.when(x < 2)
    def _():
        wait(kv.at[:, pl.ds(0, BLK)], kv_sem.at[x, 0])

    for p in range(PIECES):
        for j in (0, 1):
            @pl.when(x != j)
            def _():
                arrived(j, p)

    wait(kv.at[:, pl.ds(0, WINDOW)], halo_sem)
    wait(far.at[:, pl.ds(SUMM, FAR - SUMM)], far_sem)

    def step(s, carry):
        u = jnp.maximum(s - HEAD_DEV, 0)
        i = lax.rem(u, 3)
        other = jnp.where(i == 0, 1, jnp.where(i == 1, 3, 2))
        dx = jnp.where(s < HEAD_DEV, 0, other)
        dr = jnp.where(s < HEAD_DEV, s, u // 3)
        j = ring(-dx)
        r = piece_of(dr)
        t = j * PIECES + r
        here = rows(t * TILE, TILE)
        wait(q_all.at[pl.ds(0, PIECE)], q_sem.at[dx, dr])
        q = q_all[here, :]
        nt = (((1,), (1,)), ((), ()))
        near = rows(t * TILE, BAND)
        s_near = lax.dot_general(q, kv[0, near, :], nt, preferred_element_type=jnp.float32)
        s_far = lax.dot_general(q, far[0], nt, preferred_element_type=jnp.float32)
        col = lax.broadcasted_iota(jnp.int32, (TILE, BAND), 1)
        row = lax.broadcasted_iota(jnp.int32, (TILE, BAND), 0)
        start = jnp.where(group == 0, jnp.maximum(WINDOW - t * TILE, 0), 0)
        admitted = (col > row) & (col <= row + WINDOW) & (col >= start)
        s_near = jnp.where(admitted, s_near, LOW)
        case = jnp.where(t < 7, 0, jnp.where(t == 7, 1, 2))
        s_far = s_far + bias[case]
        top = jnp.maximum(
            jnp.max(s_near, axis=1, keepdims=True), jnp.max(s_far, axis=1, keepdims=True)
        )
        w_near = jnp.exp2((s_near - top) * EXP_SCALE)
        w_far = jnp.exp2((s_far - top) * EXP_SCALE)
        total = jnp.sum(w_near, axis=1, keepdims=True) + jnp.sum(w_far, axis=1, keepdims=True)
        mixed = jnp.dot(w_near.astype(jnp.bfloat16), kv[1, near, :], preferred_element_type=jnp.float32)
        mixed = mixed + jnp.dot(w_far.astype(jnp.bfloat16), far[1], preferred_element_type=jnp.float32)
        o_all[here, :] = (mixed / total).astype(jnp.bfloat16)
        target = out.at[:, cols(h * RING + x)]

        @pl.when(s == 0)
        def _():
            pltpu.make_async_copy(o_all.at[here], target, o_sem).start()

        @pl.when(s > 0)
        def _():
            pltpu.make_async_remote_copy(
                src_ref=o_all.at[here],
                dst_ref=target,
                send_sem=o_send,
                recv_sem=o_sem,
                device_id=(first + j, r),
                device_id_type=MESH,
            ).start()

        return carry

    lax.fori_loop(0, STEPS, step, 0)

    wait(kv.at[:, pl.ds(0, 3 * BLK)], send_sem.at[0])
    wait(q_all.at[pl.ds(0, 3 * BLK)], send_sem.at[1])
    wait(kv.at[:, pl.ds(0, WINDOW)], halo_send)
    wait(far.at[:, pl.ds(SUMM, FAR - SUMM)], far_send)
    wait(o_all.at[pl.ds(0, ROWS - TILE)], o_send)
    wait(out, o_sem)


def on_device(queries, key_rows, value_rows):
    dma = pltpu.SemaphoreType.DMA
    return pl.pallas_call(
        kernel,
        name="attention",
        out_shape=jax.ShapeDtypeStruct((BLK // HEAD_DEV, HEAD_DEV * RING * HD), jnp.bfloat16),
        in_specs=[pl.BlockSpec(memory_space=pltpu.MemorySpace.HBM)] * 3,
        out_specs=pl.BlockSpec(memory_space=pltpu.VMEM),
        scratch_shapes=[
            pltpu.VMEM((3, BLK, RING * HD), jnp.bfloat16),
            pltpu.VMEM((ROWS, HD), jnp.bfloat16),
            pltpu.VMEM((2, WINDOW + ROWS, HD), jnp.bfloat16),
            pltpu.VMEM((2, FAR, HD), jnp.bfloat16),
            pltpu.VMEM((ROWS, HD), jnp.bfloat16),
            pltpu.VMEM((3, TILE, FAR), jnp.float32),
            dma((3,)),
            dma((RING, PIECES)),
            dma((RING, PIECES)),
            dma,
            dma,
            dma,
            dma((2,)),
            dma,
            dma,
            dma,
        ],
        compiler_params=pltpu.CompilerParams(
            collective_id=1, has_side_effects=True, vmem_limit_bytes=60 << 20
        ),
    )(queries, key_rows, value_rows)


def solution(mesh):
    placed = (P("ctx", "head"), P("ctx", "head"), P("ctx", "head"))
    return jax.shard_map(
        on_device, mesh=mesh, in_specs=placed, out_specs=P(("ctx", "head"), None), check_vma=False
    )
```

time: 649 us -> 49.2 us (0.08)
  waiting for transfers between devices: 513 us -> 0 us
  blocking collectives: 58.9 us -> 0 us
  Pallas kernels: 0 us -> 46.6 us
  matrix products: 20.9 us -> 0 us
  starting transfers between devices: 16.7 us -> 0 us
  local copies, waits for them, and re-layouts: 16.3 us -> 1.88 us
  between operations: 13.6 us -> 0.01 us
  other arithmetic: 9.75 us -> 0 us
    all_gather x2 -> x0, waiting for transfers between devices: 482 us -> none  [the longest x1 281 us: on_device(): lax.all_gather(own_values, 'ctx', axis=0, tiled=True)]
    all_to_all x1 -> x0, blocking collectives: 58.9 us -> none  [on_device(): lax.all_to_all(outputs, 'head', split_axis=0, concat_axis=1, tiled=True)]
    pallas_call x0 -> x1, Pallas kernels: none -> 46.6 us  [on_device(): pl.pallas_call(kernel, name='attention', out_shape=jax.ShapeDtypeStruct((...]
    ppermute x4 -> x0, waiting for transfers between devices: 31 us -> none  [shifted(): return lax.ppermute(block, axis, route)]
    dot_general x4 -> x0, matrix products: 20.9 us -> none  [the longest x1 8.16 us: on_device(): jnp.einsum('hqk,khd->qhd', near_weights.astype(jnp.bfloat16), value_slab,...]
    ppermute x4 -> x0, starting transfers between devices: 16.7 us -> none  [shifted(): return lax.ppermute(block, axis, route)]
  transfers between devices with their start and end apart: 6 -> 0, of which waited for: 4 -> 0; matrix products, arithmetic and copies ran while one was open for 4% -> 0% of each run, Pallas kernels for 0% -> 0%
where the time goes in v1:
time: 49.2 us; the launch traced here: 48.5 us
  Pallas kernels  46.6 us (95%)
  local copies, waits for them, and re-layouts  1.88 us (4%)
    pallas_call x1, Pallas kernels, on_device(): pl.pallas_call(kernel, name='attention', out_shape=jax.ShapeDtypeStruct((...  46.6 us
    unnamed x1, local copies, waits for them, and re-layouts  1.88 us

profile of v1, /device:TPU:1, one launch (start us, length us, event | category | flops | bytes accessed | tf_op | source)
XLA Modules:
  0.0 48.5 jit_solution(3045390168763994337)
XLA Ops:
  0.0 46.6 %attention.1 = bf16[128,2048]{1,0:T(8,128)(2,1)} custom-call(bf16[512,512]{1,0:T(8,128)(2,1)} %q_in.1, bf16[512,512]{1,0:T(8,128)(2,1)} %k_in.1, bf16[512,512]{1,0:T(8,128)(2,1)} %v_in.1), custom_call_target="tpu_custom_call" | custom-call | tf_op jit(solution)/shard_map/attention/pallas_call | solution.py:229
  46.6 1.9 %copy.5 = bf16[128,2048]{1,0:T(8,128)(2,1)} copy(bf16[128,2048]{1,0:T(8,128)(2,1)} %attention.1) | data formatting | bytes 1048576

commit v2 on v1

v2 whole, which is shorter than its diff:
```python
import functools

import jax
import jax.numpy as jnp
from jax import lax
from jax.experimental import pallas as pl
from jax.experimental.pallas import tpu as pltpu
from jax.sharding import PartitionSpec as P

HD = 128
BLK = 512
RING = 4
HEAD_DEV = 4
ROWS = RING * BLK
WINDOW = 1024
SUMM = 16
GROUPS = 16
FAR_STEP = 0
FAR = GROUPS * SUMM
TILE = 256
BAND = WINDOW + TILE
STEPS = ROWS // TILE
HALF = BLK // TILE
PIECES = 4
PIECE = BLK // PIECES
PEERS = (1, 3, 2)
ORDER = (3, 2, 1, 0)
LOW = -1e30
EXP_SCALE = HD**-0.5 * 1.4426950408889634
MESH = pl.DeviceIdType.MESH


def kernel(
    q_in, k_in, v_in, out, q_all, kv, far, o_all, bias,
    kv_sem, q_sem, halo_sem, far_sem, o_sem, send_sem, halo_send, far_send, o_send,
    halo_ready, far_ready,
):
    ctx, h = lax.axis_index("ctx"), lax.axis_index("head")
    x, group = lax.rem(ctx, RING), ctx // RING
    first = ctx - x

    def ring(dx):
        return lax.rem(x + dx + RING, RING)

    layers = GROUPS // 2
    depth = lax.rem(group, layers)
    rank = 2 * depth + group // layers

    def ranked(place):
        return ((lax.rem(place, 2) * layers + place // 2) * RING + x, h)

    def group_peer(d):
        return (lax.rem(ctx + RING * d, RING * GROUPS), h)

    def cols(place):
        return pl.ds(pl.multiple_of(place * HD, HD), HD)

    def rows(start, size):
        return pl.ds(pl.multiple_of(start, PIECE), size)

    def wait(ref, sem):
        pltpu.make_async_copy(ref, ref, sem).wait()

    def half_of(d):
        return lax.rem(h // 2 + d, HALF)

    sources = ((0, k_in), (1, v_in))
    own = pl.ds(pl.multiple_of(WINDOW + x * BLK, BLK), BLK)
    for i, src in sources:
        pltpu.make_async_copy(src.at[:, cols(x)], kv.at[i, own], kv_sem.at[x, 0]).start()
    pltpu.make_async_copy(
        q_in.at[:, cols(x)], q_all.at[pl.ds(pl.multiple_of(x * BLK, BLK), BLK)], q_sem.at[0, 0]
    ).start()

    far[...] = jnp.zeros_like(far)

    @pl.when(group == 0)
    def _():
        kv[:, 0:WINDOW, :] = jnp.zeros((2, WINDOW, HD), jnp.bfloat16)

    barrier = pltpu.get_barrier_semaphore()
    partners = 0
    for dx in range(RING):
        for dh in range(HEAD_DEV):
            if dx or dh:
                pl.semaphore_signal(
                    barrier, inc=1, device_id=(first + ring(dx), lax.rem(h + dh, HEAD_DEV)),
                    device_id_type=MESH,
                )
                partners += 1
    for e in range(1, GROUPS):
        @pl.when(rank + e < GROUPS)
        def _():
            pl.semaphore_signal(barrier, inc=1, device_id=ranked(rank + e), device_id_type=MESH)

    col = lax.broadcasted_iota(jnp.int32, (TILE, FAR), 1)
    row = lax.broadcasted_iota(jnp.int32, (TILE, FAR), 0)
    known = (col >= SUMM) & (col < SUMM * (group + 1))
    for case in range(3):
        seen = known
        if case == 0:
            seen = known & (col >= 2 * SUMM)
        if case == 1:
            seen = known & ((col >= 2 * SUMM) | (col - SUMM <= row - (TILE - SUMM)))
        bias[case] = jnp.where(seen, 0.0, LOW)

    pl.semaphore_wait(barrier, partners + rank)
    for e in range(1, GROUPS):
        place = jnp.maximum(rank - e, 0)
        source = lax.rem(place, 2) * layers + place // 2

        @pl.when((e <= rank) & (source < group - 1))
        def _():
            pl.semaphore_signal(far_ready, inc=1, device_id=ranked(place), device_id_type=MESH)

        @pl.when((e <= rank) & (source == group - 1))
        def _():
            pl.semaphore_signal(halo_ready, inc=1, device_id=ranked(place), device_id_type=MESH)


    def send_kv(p):
        for dx in PEERS:
            place = ring(dx)
            for i, src in sources:
                pltpu.make_async_remote_copy(
                    src_ref=src.at[pl.ds(p * PIECE, PIECE), cols(place)],
                    dst_ref=kv.at[i, rows(WINDOW + x * BLK + p * PIECE, PIECE)],
                    send_sem=send_sem.at[0],
                    recv_sem=kv_sem.at[x, p],
                    device_id=(first + place, h),
                    device_id_type=MESH,
                ).start()

    def send_q(d):
        half = half_of(d)
        for dx in PEERS:
            place = ring(dx)
            pltpu.make_async_remote_copy(
                src_ref=q_in.at[rows(half * TILE, TILE), cols(place)],
                dst_ref=q_all.at[rows(x * BLK + half * TILE, TILE)],
                send_sem=send_sem.at[1],
                recv_sem=q_sem.at[dx, d],
                device_id=(first + place, h),
                device_id_type=MESH,
            ).start()

    rounds = [functools.partial(send_kv, p) for p in ORDER]
    rounds += [functools.partial(send_q, d) for d in range(HALF)]
    ahead = 2
    for send in rounds[:ahead]:
        send()

    def to_next(j, p):
        return pltpu.make_async_remote_copy(
            src_ref=kv.at[:, pl.ds(WINDOW + j * BLK + p * PIECE, PIECE)],
            dst_ref=kv.at[:, pl.ds((j - 2) * BLK + p * PIECE, PIECE)],
            send_sem=halo_send,
            recv_sem=halo_sem,
            device_id=group_peer(1),
            device_id_type=MESH,
        )

    def summary(d):
        return pltpu.make_async_remote_copy(
            src_ref=kv.at[:, pl.ds(WINDOW + ROWS - SUMM, SUMM)],
            dst_ref=far.at[:, pl.ds(d * SUMM, SUMM)],
            send_sem=far_send.at[d],
            recv_sem=far_sem.at[d],
            device_id=group_peer(d),
            device_id_type=MESH,
        )

    def arrived(j, p):
        wait(kv.at[:, pl.ds(0, PIECE)], kv_sem.at[j, p])

    @pl.when(x >= 2)
    def _():
        wait(kv.at[:, pl.ds(0, BLK)], kv_sem.at[x, 0])

    has_next = group < GROUPS - 1
    for step, p in enumerate(ORDER):
        for j in (3, 2):
            @pl.when(x != j)
            def _():
                arrived(j, p)

            if (step, j) == (0, 3):
                @pl.when(depth < layers - 1)
                def _():
                    pl.semaphore_wait(halo_ready, 1)

            @pl.when(has_next)
            def _():
                to_next(j, p).start()

        if step == FAR_STEP:
            later = jnp.where(group < layers, GROUPS - 1 - 2 * depth, layers - 1 - depth)

            ready = later - jnp.where(depth < layers - 1, 1, 0)

            @pl.when(ready > 0)
            def _():
                pl.semaphore_wait(far_ready, ready)

            for d in range(1, GROUPS):
                pl.when(group + d < GROUPS)(summary(d).start)
        if ahead + step < len(rounds):
            rounds[ahead + step]()
    for send in rounds[ahead + PIECES:]:
        send()
    wait(q_all.at[pl.ds(0, BLK)], q_sem.at[0, 0])

    @pl.when(x < 2)
    def _():
        wait(kv.at[:, pl.ds(0, BLK)], kv_sem.at[x, 0])

    for p in ORDER:
        for j in (0, 1):
            @pl.when(x != j)
            def _():
                arrived(j, p)

    for d in range(1, GROUPS):
        pl.when(d <= group)(functools.partial(wait, far.at[:, pl.ds(d * SUMM, SUMM)], far_sem.at[d]))

    def step(s, carry):
        u = jnp.maximum(s - 2, 0)
        i = lax.rem(u, 3)
        late_j = jnp.where(s < 2, x, jnp.where(i == 0, 5 - x, i - 1))
        late_d = jnp.where(s < 2, s, u // 3)
        i = jnp.maximum(s - 5, 0)
        early_j = jnp.where(
            s < 2, 2 + s, jnp.where(s < 4, x, jnp.where((s == 4) | (i == 2), 1 - x, 2 + i))
        )
        early_d = jnp.where((s < 2) | (s == 4), 0, jnp.where(s < 4, s - 2, 1))
        j = jnp.where(x >= 2, late_j, early_j)
        d = jnp.where(x >= 2, late_d, early_d)
        dx = lax.rem(x - j + RING, RING)
        half = half_of(d)
        t = j * HALF + half
        here = rows(t * TILE, TILE)

        @pl.when((s == jnp.where(x >= 2, 3, 2)) & (group > 0))
        def _():
            wait(kv.at[:, pl.ds(0, WINDOW)], halo_sem)

        @pl.when(dx > 0)
        def _():
            wait(q_all.at[pl.ds(0, TILE)], q_sem.at[dx, d])

        case = jnp.where(t < 3, 0, jnp.where(t == 3, 1, 2))
        outside = jnp.where(group == 0, WINDOW - t * TILE, 0)

        def attend(whole):
            q = q_all[here, :]
            nt = (((1,), (1,)), ((), ()))
            near = rows(t * TILE, BAND)
            scores = lax.dot_general(q, kv[0, near, :], nt, preferred_element_type=jnp.float32)
            s_far = lax.dot_general(q, far[0], nt, preferred_element_type=jnp.float32) + bias[case]
            col = lax.broadcasted_iota(jnp.int32, (TILE, TILE), 1)
            row = lax.broadcasted_iota(jnp.int32, (TILE, TILE), 0)
            s_old = jnp.where(col > row, scores[:, :TILE], LOW)
            s_mid = scores[:, TILE:WINDOW]
            s_new = jnp.where(col <= row, scores[:, WINDOW:], LOW)
            if not whole:
                place = lax.broadcasted_iota(jnp.int32, (TILE, WINDOW), 1)
                s_old = jnp.where(place[:, :TILE] >= outside, s_old, LOW)
                s_mid = jnp.where(place[:, TILE:] >= outside, s_mid, LOW)
            parts = [s_old, s_mid, s_new, s_far]
            tops = [jnp.max(part, axis=1, keepdims=True) for part in parts]
            top = jnp.maximum(jnp.maximum(tops[0], tops[1]), jnp.maximum(tops[2], tops[3]))
            weights = [jnp.exp2((part - top) * EXP_SCALE) for part in parts]
            total = sum(jnp.sum(part, axis=1, keepdims=True) for part in weights)
            rounded = [part.astype(jnp.bfloat16) for part in weights]
            mixed = jnp.dot(
                jnp.concatenate(rounded[:3], axis=1), kv[1, near, :], preferred_element_type=jnp.float32
            )
            mixed = mixed + jnp.dot(rounded[3], far[1], preferred_element_type=jnp.float32)
            o_all[here, :] = (mixed / total).astype(jnp.bfloat16)

        @pl.when(outside > 0)
        def _():
            attend(False)

        @pl.when(outside <= 0)
        def _():
            attend(True)

        target = out.at[:, cols(h * RING + x)]
        for e in range(2):
            r = 2 * half + lax.rem(h + e, 2)
            result = o_all.at[rows(j * BLK + r * PIECE, PIECE)]

            def send(result=result, r=r):
                pltpu.make_async_remote_copy(
                    src_ref=result,
                    dst_ref=target,
                    send_sem=o_send,
                    recv_sem=o_sem,
                    device_id=(first + j, r),
                    device_id_type=MESH,
                ).start()

            if e:
                send()
            else:
                mine = (dx == 0) & (d == 0)

                @pl.when(mine)
                def _():
                    pltpu.make_async_copy(result, target, o_sem).start()

                pl.when(jnp.logical_not(mine))(send)

        return carry

    lax.fori_loop(0, STEPS, step, 0)

    wait(kv.at[:, pl.ds(0, 3 * BLK)], send_sem.at[0])
    wait(q_all.at[pl.ds(0, 3 * BLK)], send_sem.at[1])
    pl.when(has_next)(functools.partial(wait, kv.at[:, pl.ds(0, WINDOW)], halo_send))
    for d in range(1, GROUPS):
        pl.when(group + d < GROUPS)(functools.partial(wait, far.at[:, pl.ds(d * SUMM, SUMM)], far_send.at[d]))
    wait(o_all.at[pl.ds(0, ROWS - PIECE)], o_send)
    wait(out, o_sem)


def on_device(queries, key_rows, value_rows):
    dma = pltpu.SemaphoreType.DMA
    return pl.pallas_call(
        kernel,
        name="attention",
        out_shape=jax.ShapeDtypeStruct((BLK // HEAD_DEV, HEAD_DEV * RING * HD), jnp.bfloat16),
        in_specs=[pl.BlockSpec(memory_space=pltpu.MemorySpace.HBM)] * 3,
        out_specs=pl.BlockSpec(memory_space=pltpu.MemorySpace.HBM),
        scratch_shapes=[
            pltpu.VMEM((ROWS, HD), jnp.bfloat16),
            pltpu.VMEM((2, WINDOW + ROWS, HD), jnp.bfloat16),
            pltpu.VMEM((2, FAR, HD), jnp.bfloat16),
            pltpu.VMEM((ROWS, HD), jnp.bfloat16),
            pltpu.VMEM((3, TILE, FAR), jnp.float32),
            dma((RING, PIECES)),
            dma((RING, HALF)),
            dma,
            dma((GROUPS,)),
            dma,
            dma((2,)),
            dma,
            dma((GROUPS,)),
            dma,
            pltpu.SemaphoreType.REGULAR,
            pltpu.SemaphoreType.REGULAR,
        ],
        compiler_params=pltpu.CompilerParams(
            collective_id=1, has_side_effects=True, vmem_limit_bytes=60 << 20
        ),
    )(queries, key_rows, value_rows)


def solution(mesh):
    placed = (P("ctx", "head"), P("ctx", "head"), P("ctx", "head"))
    return jax.shard_map(
        on_device, mesh=mesh, in_specs=placed, out_specs=P(("ctx", "head"), None), check_vma=False
    )
```

time: 49.2 us -> 42 us (0.85)
  the two profiles are of different devices: /device:TPU:1 before, /device:TPU:25 now
where the time goes in v2:
time: 42 us; the launch traced here: 41.9 us
  Pallas kernels  40 us (95%)
  local copies, waits for them, and re-layouts  1.88 us (4%)
    pallas_call x1, Pallas kernels, on_device(): pl.pallas_call(kernel, name='attention', out_shape=jax.ShapeDtypeStruct((...  40 us
    unnamed x1, local copies, waits for them, and re-layouts  1.88 us

profile of v2, /device:TPU:25, one launch (start us, length us, event | category | flops | bytes accessed | tf_op | source)
XLA Modules:
  0.0 41.9 jit_solution(5938972239972960715)
XLA Ops:
  0.0 40.0 %attention.1 = bf16[128,2048]{1,0:T(8,128)(2,1)} custom-call(bf16[512,512]{1,0:T(8,128)(2,1)} %q_in.1, bf16[512,512]{1,0:T(8,128)(2,1)} %k_in.1, bf16[512,512]{1,0:T(8,128)(2,1)} %v_in.1), custom_call_target="tpu_custom_call" | custom-call | tf_op jit(solution)/shard_map/attention/pallas_call | solution.py:330
  40.0 1.9 %copy.5 = bf16[128,2048]{1,0:T(8,128)(2,1)} copy(bf16[128,2048]{1,0:T(8,128)(2,1)} %attention.1) | data formatting | bytes 1048576

commit v3 on v2

--- a/solution.py
+++ b/solution.py
@@ -15,7 +15,8 @@
 WINDOW = 1024
 SUMM = 16
 GROUPS = 16
-FAR_STEP = 0
+FAR_STEP = 1
+VMEM_KIB = 54400
 FAR = GROUPS * SUMM
 TILE = 256
 BAND = WINDOW + TILE
@@ -145,15 +146,14 @@
             ).start()
 
     rounds = [functools.partial(send_kv, p) for p in ORDER]
-    rounds += [functools.partial(send_q, d) for d in range(HALF)]
-    ahead = 2
+    ahead = 4
     for send in rounds[:ahead]:
         send()
 
-    def to_next(j, p):
+    def to_next(j, start, size):
         return pltpu.make_async_remote_copy(
-            src_ref=kv.at[:, pl.ds(WINDOW + j * BLK + p * PIECE, PIECE)],
-            dst_ref=kv.at[:, pl.ds((j - 2) * BLK + p * PIECE, PIECE)],
+            src_ref=kv.at[:, rows(WINDOW + j * BLK + start, size)],
+            dst_ref=kv.at[:, rows((j - 2) * BLK + start, size)],
             send_sem=halo_send,
             recv_sem=halo_sem,
             device_id=group_peer(1),
@@ -173,29 +173,35 @@
     def arrived(j, p):
         wait(kv.at[:, pl.ds(0, PIECE)], kv_sem.at[j, p])
 
+    has_next = group < GROUPS - 1
+
+    @pl.when(depth < layers - 1)
+    def _():
+        pl.semaphore_wait(halo_ready, 1)
+
     @pl.when(x >= 2)
     def _():
         wait(kv.at[:, pl.ds(0, BLK)], kv_sem.at[x, 0])
 
-    has_next = group < GROUPS - 1
+        @pl.when(has_next)
+        def _():
+            to_next(x, 0, BLK).start()
+
     for step, p in enumerate(ORDER):
         for j in (3, 2):
             @pl.when(x != j)
             def _():
                 arrived(j, p)
 
-            if (step, j) == (0, 3):
-                @pl.when(depth < layers - 1)
-                def _():
-                    pl.semaphore_wait(halo_ready, 1)
-
-            @pl.when(has_next)
+            @pl.when(has_next & (x != j))
             def _():
-                to_next(j, p).start()
-
+                to_next(j, p * PIECE, PIECE).start()
+
+        if step == 0:
+            for d in range(1, GROUPS):
+                pl.when((group + d < GROUPS) & (lax.rem(group + d, layers) < depth))(summary(d).start)
         if step == FAR_STEP:
             later = jnp.where(group < layers, GROUPS - 1 - 2 * depth, layers - 1 - depth)
-
             ready = later - jnp.where(depth < layers - 1, 1, 0)
 
             @pl.when(ready > 0)
@@ -203,11 +209,10 @@
                 pl.semaphore_wait(far_ready, ready)
 
             for d in range(1, GROUPS):
-                pl.when(group + d < GROUPS)(summary(d).start)
+                pl.when((group + d < GROUPS) & (lax.rem(group + d, layers) >= depth))(summary(d).start)
         if ahead + step < len(rounds):
             rounds[ahead + step]()
-    for send in rounds[ahead + PIECES:]:
-        send()
+    send_q(0)
     wait(q_all.at[pl.ds(0, BLK)], q_sem.at[0, 0])
 
     @pl.when(x < 2)
@@ -220,8 +225,11 @@
             def _():
                 arrived(j, p)
 
+    send_q(1)
     for d in range(1, GROUPS):
         pl.when(d <= group)(functools.partial(wait, far.at[:, pl.ds(d * SUMM, SUMM)], far_sem.at[d]))
+
+    patient = group == layers
 
     def step(s, carry):
         u = jnp.maximum(s - 2, 0)
@@ -233,14 +241,23 @@
             s < 2, 2 + s, jnp.where(s < 4, x, jnp.where((s == 4) | (i == 2), 1 - x, 2 + i))
         )
         early_d = jnp.where((s < 2) | (s == 4), 0, jnp.where(s < 4, s - 2, 1))
-        j = jnp.where(x >= 2, late_j, early_j)
-        d = jnp.where(x >= 2, late_d, early_d)
+        u = jnp.maximum(s - 4, 0)
+        last_j = jnp.where(
+            x >= 2, jnp.where(s < 2, x, jnp.where(s < 4, 5 - x, lax.rem(u, 2))),
+            jnp.where(s < 4, 2 + lax.rem(s, 2), jnp.where(s < 6, x, 1 - x)),
+        )
+        last_d = jnp.where(
+            x >= 2, jnp.where(s < 4, lax.rem(s, 2), u // 2),
+            jnp.where(s < 4, s // 2, lax.rem(s, 2)),
+        )
+        j = jnp.where(patient, last_j, jnp.where(x >= 2, late_j, early_j))
+        d = jnp.where(patient, last_d, jnp.where(x >= 2, late_d, early_d))
         dx = lax.rem(x - j + RING, RING)
         half = half_of(d)
         t = j * HALF + half
         here = rows(t * TILE, TILE)
 
-        @pl.when((s == jnp.where(x >= 2, 3, 2)) & (group > 0))
+        @pl.when((s == jnp.where(patient, 4, jnp.where(x >= 2, 3, 2))) & (group > 0))
         def _():
             wait(kv.at[:, pl.ds(0, WINDOW)], halo_sem)
 
@@ -332,7 +349,7 @@
         name="attention",
         out_shape=jax.ShapeDtypeStruct((BLK // HEAD_DEV, HEAD_DEV * RING * HD), jnp.bfloat16),
         in_specs=[pl.BlockSpec(memory_space=pltpu.MemorySpace.HBM)] * 3,
-        out_specs=pl.BlockSpec(memory_space=pltpu.MemorySpace.HBM),
+        out_specs=pl.BlockSpec(memory_space=pltpu.VMEM),
         scratch_shapes=[
             pltpu.VMEM((ROWS, HD), jnp.bfloat16),
             pltpu.VMEM((2, WINDOW + ROWS, HD), jnp.bfloat16),
@@ -352,7 +369,7 @@
             pltpu.SemaphoreType.REGULAR,
         ],
         compiler_params=pltpu.CompilerParams(
-            collective_id=1, has_side_effects=True, vmem_limit_bytes=60 << 20
+            collective_id=1, has_side_effects=True, vmem_limit_bytes=VMEM_KIB << 10
         ),
     )(queries, key_rows, value_rows)
 

time: 42 us -> 38.6 us (0.919)
  the two profiles are of different devices: /device:TPU:25 before, /device:TPU:1 now
where the time goes in v3:
time: 38.6 us; the launch traced here: 38 us
  Pallas kernels  37.2 us (96%)
  local copies, waits for them, and re-layouts  0.8 us (2%)
    pallas_call x1, Pallas kernels, on_device(): pl.pallas_call(kernel, name='attention', out_shape=jax.ShapeDtypeStruct((...  37.2 us
    unnamed x1, local copies, waits for them, and re-layouts  0.8 us

profile of v3, /device:TPU:1, one launch (start us, length us, event | category | flops | bytes accessed | tf_op | source)
XLA Modules:
  0.0 38.0 jit_solution(18168732530470545536)
XLA Ops:
  0.0 37.2 %attention.1 = bf16[128,2048]{1,0:T(8,128)(2,1)S(1)} custom-call(bf16[512,512]{1,0:T(8,128)(2,1)} %q_in.1, bf16[512,512]{1,0:T(8,128)(2,1)} %k_in.1, bf16[512,512]{1,0:T(8,128)(2,1)} %v_in.1), custom_call_target="tpu_custom_call" | custom-call | tf_op jit(solution)/shard_map/attention/pallas_call | solution.py:347
  37.2 0.8 %copy.5 = bf16[128,2048]{1,0:T(8,128)(2,1)} copy(bf16[128,2048]{1,0:T(8,128)(2,1)S(1)} %attention.1) | data formatting | bytes 1048576

commit v4 on v3

--- a/solution.py
+++ b/solution.py
@@ -15,7 +15,7 @@
 WINDOW = 1024
 SUMM = 16
 GROUPS = 16
-FAR_STEP = 1
+FAR_STEP = 2
 VMEM_KIB = 54400
 FAR = GROUPS * SUMM
 TILE = 256
@@ -25,7 +25,9 @@
 PIECES = 4
 PIECE = BLK // PIECES
 PEERS = (1, 3, 2)
-ORDER = (3, 2, 1, 0)
+PARTS = 8
+PART = BLK // PARTS
+ORDER = tuple(reversed(range(PARTS)))
 LOW = -1e30
 EXP_SCALE = HD**-0.5 * 1.4426950408889634
 MESH = pl.DeviceIdType.MESH
@@ -46,6 +48,7 @@
     layers = GROUPS // 2
     depth = lax.rem(group, layers)
     rank = 2 * depth + group // layers
+    flip = jnp.where(depth > 0, 1, 0)
 
     def ranked(place):
         return ((lax.rem(place, 2) * layers + place // 2) * RING + x, h)
@@ -57,13 +60,13 @@
         return pl.ds(pl.multiple_of(place * HD, HD), HD)
 
     def rows(start, size):
-        return pl.ds(pl.multiple_of(start, PIECE), size)
+        return pl.ds(pl.multiple_of(start, PART), size)
 
     def wait(ref, sem):
         pltpu.make_async_copy(ref, ref, sem).wait()
 
     def half_of(d):
-        return lax.rem(h // 2 + d, HALF)
+        return lax.rem(h // 2 + flip + d, HALF)
 
     sources = ((0, k_in), (1, v_in))
     own = pl.ds(pl.multiple_of(WINDOW + x * BLK, BLK), BLK)
@@ -106,26 +109,14 @@
         bias[case] = jnp.where(seen, 0.0, LOW)
 
     pl.semaphore_wait(barrier, partners + rank)
-    for e in range(1, GROUPS):
-        place = jnp.maximum(rank - e, 0)
-        source = lax.rem(place, 2) * layers + place // 2
-
-        @pl.when((e <= rank) & (source < group - 1))
-        def _():
-            pl.semaphore_signal(far_ready, inc=1, device_id=ranked(place), device_id_type=MESH)
-
-        @pl.when((e <= rank) & (source == group - 1))
-        def _():
-            pl.semaphore_signal(halo_ready, inc=1, device_id=ranked(place), device_id_type=MESH)
-
 
     def send_kv(p):
         for dx in PEERS:
             place = ring(dx)
             for i, src in sources:
                 pltpu.make_async_remote_copy(
-                    src_ref=src.at[pl.ds(p * PIECE, PIECE), cols(place)],
-                    dst_ref=kv.at[i, rows(WINDOW + x * BLK + p * PIECE, PIECE)],
+                    src_ref=src.at[pl.ds(p * PART, PART), cols(place)],
+                    dst_ref=kv.at[i, rows(WINDOW + x * BLK + p * PART, PART)],
                     send_sem=send_sem.at[0],
                     recv_sem=kv_sem.at[x, p],
                     device_id=(first + place, h),
@@ -150,6 +141,18 @@
     for send in rounds[:ahead]:
         send()
 
+    for e in range(1, GROUPS):
+        place = jnp.maximum(rank - e, 0)
+        source = lax.rem(place, 2) * layers + place // 2
+
+        @pl.when((e <= rank) & (source < group - 1))
+        def _():
+            pl.semaphore_signal(far_ready, inc=1, device_id=ranked(place), device_id_type=MESH)
+
+        @pl.when((e <= rank) & (source == group - 1))
+        def _():
+            pl.semaphore_signal(halo_ready, inc=1, device_id=ranked(place), device_id_type=MESH)
+
     def to_next(j, start, size):
         return pltpu.make_async_remote_copy(
             src_ref=kv.at[:, rows(WINDOW + j * BLK + start, size)],
@@ -171,7 +174,7 @@
         )
 
     def arrived(j, p):
-        wait(kv.at[:, pl.ds(0, PIECE)], kv_sem.at[j, p])
+        wait(kv.at[:, pl.ds(0, PART)], kv_sem.at[j, p])
 
     has_next = group < GROUPS - 1
 
@@ -195,7 +198,7 @@
 
             @pl.when(has_next & (x != j))
             def _():
-                to_next(j, p * PIECE, PIECE).start()
+                to_next(j, p * PART, PART).start()
 
         if step == 0:
             for d in range(1, GROUPS):
@@ -230,21 +233,23 @@
         pl.when(d <= group)(functools.partial(wait, far.at[:, pl.ds(d * SUMM, SUMM)], far_sem.at[d]))
 
     patient = group == layers
+    odd = lax.rem(x, 2)
 
     def step(s, carry):
         u = jnp.maximum(s - 2, 0)
         i = lax.rem(u, 3)
-        late_j = jnp.where(s < 2, x, jnp.where(i == 0, 5 - x, i - 1))
+        late_j = jnp.where(s < 2, x, jnp.where(i == 0, 5 - x, lax.rem(i + 1 + odd, 2)))
         late_d = jnp.where(s < 2, s, u // 3)
         i = jnp.maximum(s - 5, 0)
         early_j = jnp.where(
-            s < 2, 2 + s, jnp.where(s < 4, x, jnp.where((s == 4) | (i == 2), 1 - x, 2 + i))
+            s < 2, 2 + lax.rem(s + odd, 2),
+            jnp.where(s < 4, x, jnp.where((s == 4) | (i == 2), 1 - x, 2 + lax.rem(i + odd, 2))),
         )
         early_d = jnp.where((s < 2) | (s == 4), 0, jnp.where(s < 4, s - 2, 1))
         u = jnp.maximum(s - 4, 0)
         last_j = jnp.where(
-            x >= 2, jnp.where(s < 2, x, jnp.where(s < 4, 5 - x, lax.rem(u, 2))),
-            jnp.where(s < 4, 2 + lax.rem(s, 2), jnp.where(s < 6, x, 1 - x)),
+            x >= 2, jnp.where(s < 2, x, jnp.where(s < 4, 5 - x, lax.rem(u + odd, 2))),
+            jnp.where(s < 4, 2 + lax.rem(s + odd, 2), jnp.where(s < 6, x, 1 - x)),
         )
         last_d = jnp.where(
             x >= 2, jnp.where(s < 4, lax.rem(s, 2), u // 2),
@@ -271,28 +276,28 @@
         def attend(whole):
             q = q_all[here, :]
             nt = (((1,), (1,)), ((), ()))
-            near = rows(t * TILE, BAND)
+            skip = 0 if whole else TILE
+            near = rows(t * TILE + skip, BAND - skip)
             scores = lax.dot_general(q, kv[0, near, :], nt, preferred_element_type=jnp.float32)
             s_far = lax.dot_general(q, far[0], nt, preferred_element_type=jnp.float32) + bias[case]
             col = lax.broadcasted_iota(jnp.int32, (TILE, TILE), 1)
             row = lax.broadcasted_iota(jnp.int32, (TILE, TILE), 0)
-            s_old = jnp.where(col > row, scores[:, :TILE], LOW)
-            s_mid = scores[:, TILE:WINDOW]
-            s_new = jnp.where(col <= row, scores[:, WINDOW:], LOW)
-            if not whole:
-                place = lax.broadcasted_iota(jnp.int32, (TILE, WINDOW), 1)
-                s_old = jnp.where(place[:, :TILE] >= outside, s_old, LOW)
-                s_mid = jnp.where(place[:, TILE:] >= outside, s_mid, LOW)
-            parts = [s_old, s_mid, s_new, s_far]
-            tops = [jnp.max(part, axis=1, keepdims=True) for part in parts]
-            top = jnp.maximum(jnp.maximum(tops[0], tops[1]), jnp.maximum(tops[2], tops[3]))
+            s_mid = scores[:, TILE - skip : WINDOW - skip]
+            s_new = jnp.where(col <= row, scores[:, WINDOW - skip :], LOW)
+            if whole:
+                s_old = jnp.where(col > row, scores[:, :TILE], LOW)
+                parts = [s_old, s_mid, s_new, s_far]
+            else:
+                place = lax.broadcasted_iota(jnp.int32, (1, WINDOW - TILE), 1) + TILE
+                parts = [s_mid + jnp.where(place >= outside, 0.0, LOW), s_new, s_far]
+            top = functools.reduce(jnp.maximum, [jnp.max(part, axis=1, keepdims=True) for part in parts])
             weights = [jnp.exp2((part - top) * EXP_SCALE) for part in parts]
             total = sum(jnp.sum(part, axis=1, keepdims=True) for part in weights)
             rounded = [part.astype(jnp.bfloat16) for part in weights]
             mixed = jnp.dot(
-                jnp.concatenate(rounded[:3], axis=1), kv[1, near, :], preferred_element_type=jnp.float32
+                jnp.concatenate(rounded[:-1], axis=1), kv[1, near, :], preferred_element_type=jnp.float32
             )
-            mixed = mixed + jnp.dot(rounded[3], far[1], preferred_element_type=jnp.float32)
+            mixed = mixed + jnp.dot(rounded[-1], far[1], preferred_element_type=jnp.float32)
             o_all[here, :] = (mixed / total).astype(jnp.bfloat16)
 
         @pl.when(outside > 0)
@@ -321,7 +326,7 @@
             if e:
                 send()
             else:
-                mine = (dx == 0) & (d == 0)
+                mine = (dx == 0) & (d == flip)
 
                 @pl.when(mine)
                 def _():
@@ -356,7 +361,7 @@
             pltpu.VMEM((2, FAR, HD), jnp.bfloat16),
             pltpu.VMEM((ROWS, HD), jnp.bfloat16),
             pltpu.VMEM((3, TILE, FAR), jnp.float32),
-            dma((RING, PIECES)),
+            dma((RING, PARTS)),
             dma((RING, HALF)),
             dma,
             dma((GROUPS,)),

time: 38.6 us -> 38.4 us (level)
  no operation moved by 1% of the time
where the time goes in v4:
time: 38.4 us; the launch traced here: 37.9 us
  Pallas kernels  37.1 us (97%)
  local copies, waits for them, and re-layouts  0.8 us (2%)
    pallas_call x1, Pallas kernels, on_device(): pl.pallas_call(kernel, name='attention', out_shape=jax.ShapeDtypeStruct((...  37.1 us
    unnamed x1, local copies, waits for them, and re-layouts  0.8 us

profile of v4, /device:TPU:1, one launch (start us, length us, event | category | flops | bytes accessed | tf_op | source)
XLA Modules:
  0.0 37.9 jit_solution(7041118556335481189)
XLA Ops:
  0.0 37.1 %attention.1 = bf16[128,2048]{1,0:T(8,128)(2,1)S(1)} custom-call(bf16[512,512]{1,0:T(8,128)(2,1)} %q_in.1, bf16[512,512]{1,0:T(8,128)(2,1)} %k_in.1, bf16[512,512]{1,0:T(8,128)(2,1)} %v_in.1), custom_call_target="tpu_custom_call" | custom-call | tf_op jit(solution)/shard_map/attention/pallas_call | solution.py:352
  37.1 0.8 %copy.5 = bf16[128,2048]{1,0:T(8,128)(2,1)} copy(bf16[128,2048]{1,0:T(8,128)(2,1)S(1)} %attention.1) | data formatting | bytes 1048576

commit v5 on v4

--- a/solution.py
+++ b/solution.py
@@ -213,9 +213,11 @@
 
             for d in range(1, GROUPS):
                 pl.when((group + d < GROUPS) & (lax.rem(group + d, layers) >= depth))(summary(d).start)
+        if step == 5:
+            pl.when(group != layers - 1)(functools.partial(send_q, 0))
         if ahead + step < len(rounds):
             rounds[ahead + step]()
-    send_q(0)
+    pl.when(group == layers - 1)(functools.partial(send_q, 0))
     wait(q_all.at[pl.ds(0, BLK)], q_sem.at[0, 0])
 
     @pl.when(x < 2)
@@ -252,8 +254,8 @@
             jnp.where(s < 4, 2 + lax.rem(s + odd, 2), jnp.where(s < 6, x, 1 - x)),
         )
         last_d = jnp.where(
-            x >= 2, jnp.where(s < 4, lax.rem(s, 2), u // 2),
-            jnp.where(s < 4, s // 2, lax.rem(s, 2)),
+            x >= 2, jnp.where(s < 4, lax.rem(s, 2), 1 - u // 2),
+            jnp.where(s < 4, s // 2, 1 - lax.rem(s, 2)),
         )
         j = jnp.where(patient, last_j, jnp.where(x >= 2, late_j, early_j))
         d = jnp.where(patient, last_d, jnp.where(x >= 2, late_d, early_d))

time: 38.4 us -> 36.8 us (0.958)
  Pallas kernels: 37.1 us -> 35.9 us
    pallas_call x1, Pallas kernels: 37.1 us -> 35.9 us  [on_device(): pl.pallas_call(kernel, name='attention', out_shape=jax.ShapeDtypeStruct((...]
where the time goes in v5:
time: 36.8 us; the launch traced here: 36.7 us
  Pallas kernels  35.9 us (98%)
  local copies, waits for them, and re-layouts  0.8 us (2%)
    pallas_call x1, Pallas kernels, on_device(): pl.pallas_call(kernel, name='attention', out_shape=jax.ShapeDtypeStruct((...  35.9 us
    unnamed x1, local copies, waits for them, and re-layouts  0.8 us

profile of v5, /device:TPU:1, one launch (start us, length us, event | category | flops | bytes accessed | tf_op | source)
XLA Modules:
  0.0 36.7 jit_solution(9628210728525566955)
XLA Ops:
  0.0 35.9 %attention.1 = bf16[128,2048]{1,0:T(8,128)(2,1)S(1)} custom-call(bf16[512,512]{1,0:T(8,128)(2,1)} %q_in.1, bf16[512,512]{1,0:T(8,128)(2,1)} %k_in.1, bf16[512,512]{1,0:T(8,128)(2,1)} %v_in.1), custom_call_target="tpu_custom_call" | custom-call | tf_op jit(solution)/shard_map/attention/pallas_call | solution.py:354
  35.9 0.8 %copy.5 = bf16[128,2048]{1,0:T(8,128)(2,1)} copy(bf16[128,2048]{1,0:T(8,128)(2,1)S(1)} %attention.1) | data formatting | bytes 1048576

commit v6 on v5

--- a/solution.py
+++ b/solution.py
@@ -213,7 +213,7 @@
 
             for d in range(1, GROUPS):
                 pl.when((group + d < GROUPS) & (lax.rem(group + d, layers) >= depth))(summary(d).start)
-        if step == 5:
+        if step == 3:
             pl.when(group != layers - 1)(functools.partial(send_q, 0))
         if ahead + step < len(rounds):
             rounds[ahead + step]()

time: 36.8 us -> 37.8 us (1.027)
  Pallas kernels: 35.9 us -> 36.9 us
    pallas_call x1, Pallas kernels: 35.9 us -> 36.9 us  [on_device(): pl.pallas_call(kernel, name='attention', out_shape=jax.ShapeDtypeStruct((...]
where the time goes in v6:
time: 37.8 us; the launch traced here: 37.7 us
  Pallas kernels  36.9 us (98%)
  local copies, waits for them, and re-layouts  0.8 us (2%)
    pallas_call x1, Pallas kernels, on_device(): pl.pallas_call(kernel, name='attention', out_shape=jax.ShapeDtypeStruct((...  36.9 us
    unnamed x1, local copies, waits for them, and re-layouts  0.8 us

profile of v6, /device:TPU:1, one launch (start us, length us, event | category | flops | bytes accessed | tf_op | source)
XLA Modules:
  0.0 37.7 jit_solution(13745500138306500866)
XLA Ops:
  0.0 36.9 %attention.1 = bf16[128,2048]{1,0:T(8,128)(2,1)S(1)} custom-call(bf16[512,512]{1,0:T(8,128)(2,1)} %q_in.1, bf16[512,512]{1,0:T(8,128)(2,1)} %k_in.1, bf16[512,512]{1,0:T(8,128)(2,1)} %v_in.1), custom_call_target="tpu_custom_call" | custom-call | tf_op jit(solution)/shard_map/attention/pallas_call | solution.py:354
  36.9 0.8 %copy.5 = bf16[128,2048]{1,0:T(8,128)(2,1)} copy(bf16[128,2048]{1,0:T(8,128)(2,1)S(1)} %attention.1) | data formatting | bytes 1048576
